TPU v7x, 32 devices: a whole 2x2x4 slice. The times are simulated.
32 devices in a mesh: dp: 2 (over core), expert: 16 (over z, y, x).
Axes of the slice: x: 2, y: 2, z: 4, core: 2. Of those that a mesh axis runs over, the one named last changes fastest.
Arguments:
- tokens: bfloat16 [2048, 2560], P(('dp', 'expert')), may hold values from -6 to 6
- cotangent: bfloat16 [2048, 2560], P(('dp', 'expert')), may hold values from -0.59765625 to 0.59765625
- w_gate: bfloat16 [16, 2560, 768], P('expert', 'dp'), may hold values from -0.125 to 0.125
- w_up: bfloat16 [16, 2560, 768], P('expert', 'dp'), may hold values from -0.125 to 0.125
- expert_ids: int32 [2048, 6], P(('dp', 'expert')), may hold values from 0 to 15, all different within a row; in each aligned block of 64 rows (0 to 63, 64 to 127, ...) at most 30 rows name the same one
- gate_num: int32 [2048, 6], P(('dp', 'expert')), may hold values from 1 to 64
- swap_flags: int32 [8], replicated, may hold values 0 or 1
Outputs:
- grad_held: float32 [16, 768, 2560], P('expert', 'dp')
Inputs may be any that keep to these rules, and one draw needn't show every extreme that they name: `expert_ids`: each row names 6 different experts; the 64 rows of one device name no expert more than 30 times, a bound that some block reaches.
All inputs are finite; a program needn't handle non-finite values.
Results may differ from a plain program's by a relative error of at most 0.015.
Values may be sent and summed in bfloat16 or wider, within the bound.
A program may use at most 64 MiB of HBM per device.

v0:
```python
import jax
import jax.numpy as jnp
from jax import lax
from jax.sharding import PartitionSpec as P


def from_partner(value, axis, apart):
    return lax.ppermute(value, axis, [(i, i ^ 1 << apart) for i in range(lax.axis_size(axis))])


def shards(tokens, cotangent, w_gate, w_up, expert_ids, gate_num, swap_flags):
    expert_count = lax.axis_size("expert")
    half_count = expert_count // 2
    swap_bit = expert_count.bit_length() - 2
    my_index = lax.axis_index("expert")
    tok_count, top_count = expert_ids.shape
    capacity = 5 * tok_count * top_count // (4 * expert_count)
    width = tokens.shape[1]
    my_flag = swap_flags[my_index % half_count] == 1
    flat_ids = expert_ids.reshape(-1)
    destination = jnp.where(
        swap_flags[flat_ids % half_count] == 1, (flat_ids + half_count) % expert_count, flat_ids
    )
    columns = jnp.arange(expert_count, dtype=jnp.int32)
    one_hot = (destination[:, None] == columns[None, :]).astype(jnp.int32)
    ranking = jnp.sum((jnp.cumsum(one_hot, axis=0) - one_hot) * one_hot, axis=1)
    slot = destination * capacity + ranking
    slot_ids = jnp.arange(expert_count * capacity, dtype=jnp.int32)
    picked = (slot_ids[:, None] == slot[None, :]).reshape(
        expert_count * capacity, tok_count, top_count
    )
    token_map = jnp.sum(picked.astype(jnp.int32), axis=2).astype(jnp.bfloat16)
    fractions = gate_num.astype(jnp.float32) / 64.0
    weight_map = jnp.sum(jnp.where(picked, fractions[None], 0.0), axis=2).astype(jnp.bfloat16)
    send_rows = jnp.dot(token_map, tokens, preferred_element_type=jnp.float32).astype(jnp.bfloat16)
    send_grads = jnp.dot(weight_map, cotangent, preferred_element_type=jnp.float32).astype(
        jnp.bfloat16
    )
    send_rows = send_rows.reshape(expert_count, capacity, width)
    send_grads = send_grads.reshape(expert_count, capacity, width)
    recv_rows, recv_grads = (
        lax.all_to_all(send_rows, "expert", split_axis=0, concat_axis=0, tiled=True),
        lax.all_to_all(send_grads, "expert", split_axis=0, concat_axis=0, tiled=True),
    )
    recv_rows = recv_rows.reshape(expert_count * capacity, width)
    recv_grads = recv_grads.reshape(expert_count * capacity, width)
    gate_rows = w_gate[0]
    up_rows = w_up[0]
    other_gate, other_up = from_partner((gate_rows, up_rows), "expert", swap_bit)
    gate_rows = jnp.where(my_flag, other_gate, gate_rows)
    up_rows = jnp.where(my_flag, other_up, up_rows)
    gate_sum = jnp.dot(
        recv_rows,
        lax.all_gather(gate_rows, "dp", axis=0, tiled=True),
        preferred_element_type=jnp.float32,
    )
    up_sum = jnp.dot(
        recv_rows,
        lax.all_gather(up_rows, "dp", axis=0, tiled=True),
        preferred_element_type=jnp.float32,
    )
    hidden = (jax.nn.silu(gate_sum) * up_sum).astype(jnp.bfloat16)
    grads = lax.psum_scatter(
        lax.dot_general(
            hidden, recv_grads, (((0,), (0,)), ((), ())), preferred_element_type=jnp.float32
        ).astype(jnp.bfloat16),
        "dp",
        scatter_dimension=0,
        tiled=True,
    ).astype(jnp.float32)
    return grads[None]


def solution(mesh):
    in_specs = (
        P(("dp", "expert"), None),
        P(("dp", "expert"), None),
        P("expert", "dp", None),
        P("expert", "dp", None),
        P(("dp", "expert"), None),
        P(("dp", "expert"), None),
        P(),
    )
    out_specs = P("expert", "dp", None)
    return jax.shard_map(shards, mesh=mesh, in_specs=in_specs, out_specs=out_specs, check_vma=False)
```

profile of v0, /device:TPU:0, one launch (start us, length us, event | category | flops | bytes accessed | tf_op | source)
XLA Modules:
  0.0 336.4 jit_solution(1926700044830341601)
XLA Ops:
  6.5 0.0 copy-start
  6.5 4.0 %collective-permute-start = (bf16[1280,768]{1,0:T(8,128)(2,1)}, bf16[1280,768]{1,0:T(8,128)(2,1)}, u32[]{:S(2)}, u32[]{:S(2)}) collective-permute-start(bf16[1280,768]{1,0:T(8,128)(2,1)} %bitcast.46), channel_id=1, source_target_pairs={{0,8},{1,9},{2,10},{3,11},{4,12},{5,13},{6,14},{7,15},{8,0},{9,1},... | collective-permute-start | bytes 5898248 | tf_op jit(solution)/shard_map/ppermute | solution.py:8
  10.6 0.8 copy.17
  11.3 0.1 reshape.165
  11.5 0.1 reshape.166
  11.6 0.1 reshape.167
  11.8 1.7 fusion.19
  13.4 4.4 %fusion.16 = (s32[384]{0:T(512)S(1)}, s32[384,1]{0,1:T(1,128)S(1)}) fusion(s32[]{:T(128)} %bitcast.1, s32[]{:T(128)} %bitcast.2, s32[]{:T(128)} %bitcast.3, s32[]{:T(128)} %bitcast.4, s32[]{:T(128)} %bitcast.5, s32[]{:T(128)} %bitcast.7, s32[]{:T(128)} %bitcast.6, s32[384,1]{0,1:T(1,128)S(1)} %reshape.165), kind=kLoop, calls=%fused_computation.53 | loop fusion | flops 9984 | bytes 4636 | tf_op jit(solution)/shard_map/gather | solution.py:22
  17.9 0.6 fusion.13
  18.5 0.9 reduce-window.6
  19.4 0.2 slice_reduce_fusion
  19.6 0.1 fusion.10
  19.7 0.2 eq.70
  19.9 0.1 reduce_sum.30
  20.1 0.1 copy.23
  20.1 0.2 convert_reduce_fusion
  20.3 0.0 copy-done
  20.3 0.8 convolution_convert_fusion.2
  21.1 2.3 reshape.169
  23.4 4.8 %all-to-all-start = ((bf16[16,30,2560]{2,1,0:T(8,128)(2,1)}), bf16[16,30,2560]{2,1,0:T(8,128)(2,1)S(1)}, u32[]{:S(2)}, u32[]{:S(2)}) async-start(bf16[16,30,2560]{2,1,0:T(8,128)(2,1)} %reshape.169), calls=%async_computation | async-start | bytes 5242880 | tf_op jit(solution)/shard_map/all_to_all | solution.py:42
  28.3 0.0 all-gather.3.cloned.1.call-start
  29.0 95.8 %collective-permute-done = bf16[1280,768]{1,0:T(8,128)(2,1)} collective-permute-done((bf16[1280,768]{1,0:T(8,128)(2,1)}, bf16[1280,768]{1,0:T(8,128)(2,1)}, u32[]{:S(2)}, u32[]{:S(2)}) %collective-permute-start) | collective-permute-done | bytes 1966112 | tf_op jit(solution)/shard_map/ppermute | solution.py:8
  124.8 0.0 copy-start.3
  124.8 0.0 copy-start.2
  124.8 3.7 %broadcast_select_fusion.1 = bf16[1280,768]{1,0:T(8,128)(2,1)} fusion(bf16[1280,768]{1,0:T(8,128)(2,1)} %collective-permute-done, pred[]{:T(512)} %bitcast.10, bf16[1,1280,768]{2,1,0:T(8,128)(2,1)} %param.9), kind=kLoop, calls=%fused_computation.5 | loop fusion | flops 983040 | bytes 5898241 | tf_op jit(solution)/shard_map/jit(_where)/select_n | solution.py:50
  128.4 0.0 all-gather.3.cloned.1.call-update
  128.4 0.1 collective-permute-start.1
  128.5 0.0 copy-done.3
  128.5 0.2 select_reduce_fusion
  128.7 0.0 copy-done.2
  128.7 2.3 convolution_convert_fusion.1
  131.1 4.2 %reshape.171 = bf16[16,30,2560]{2,1,0:T(8,128)(2,1)} reshape(bf16[480,2560]{1,0:T(8,128)(2,1)} %convolution_convert_fusion.1) | data formatting | bytes 4915200 | tf_op jit(solution)/shard_map/reshape | solution.py:40
  135.3 51.3 %all-to-all-done = bf16[16,30,2560]{2,1,0:T(8,128)(2,1)S(1)} async-done(((bf16[16,30,2560]{2,1,0:T(8,128)(2,1)}), bf16[16,30,2560]{2,1,0:T(8,128)(2,1)S(1)}, u32[]{:S(2)}, u32[]{:S(2)}) %all-to-all-start) | async-done | bytes 2457632 | tf_op jit(solution)/shard_map/all_to_all | solution.py:42
  186.6 14.4 %all-to-all-start.1 = ((bf16[16,30,2560]{2,1,0:T(8,128)(2,1)}), bf16[16,30,2560]{2,1,0:T(8,128)(2,1)}, u32[]{:S(2)}, u32[]{:S(2)}) async-start(bf16[16,30,2560]{2,1,0:T(8,128)(2,1)} %reshape.171), calls=%async_computation.1 | async-start | bytes 5242880 | tf_op jit(solution)/shard_map/all_to_all | solution.py:43
  200.9 0.0 all-gather.5.cloned.1.call-start
  201.0 64.3 %collective-permute-done.1 = bf16[1280,768]{1,0:T(8,128)(2,1)} collective-permute-done((bf16[1280,768]{1,0:T(8,128)(2,1)}, bf16[1280,768]{1,0:T(8,128)(2,1)}, u32[]{:S(2)}, u32[]{:S(2)}) %collective-permute-start.1) | collective-permute-done | bytes 1966112 | tf_op jit(solution)/shard_map/ppermute | solution.py:8
  265.3 3.6 %broadcast_select_fusion = bf16[1280,768]{1,0:T(8,128)(2,1)} fusion(bf16[1280,768]{1,0:T(8,128)(2,1)} %collective-permute-done.1, pred[]{:T(512)} %bitcast.10, bf16[1,1280,768]{2,1,0:T(8,128)(2,1)} %param.10), kind=kLoop, calls=%fused_computation.4 | loop fusion | flops 983040 | bytes 5898241 | tf_op jit(solution)/shard_map/jit(_where)/select_n | solution.py:51
  268.9 0.0 all-gather.5.cloned.1.call-update
  268.9 0.0 reduce-scatter.2.cloned.1.call-start
  269.0 2.3 reshape.170
  271.3 0.0 copy-start.1
  271.3 13.8 %all-to-all-done.1 = bf16[16,30,2560]{2,1,0:T(8,128)(2,1)} async-done(((bf16[16,30,2560]{2,1,0:T(8,128)(2,1)}), bf16[16,30,2560]{2,1,0:T(8,128)(2,1)}, u32[]{:S(2)}, u32[]{:S(2)}) %all-to-all-start.1) | async-done | bytes 2457632 | tf_op jit(solution)/shard_map/all_to_all | solution.py:43
  285.1 4.2 %reshape.172 = bf16[480,2560]{1,0:T(8,128)(2,1)} reshape(bf16[16,30,2560]{2,1,0:T(8,128)(2,1)} %all-to-all-done.1) | data formatting | bytes 4915200 | tf_op jit(solution)/shard_map/reshape | solution.py:46
  289.3 0.0 all-gather.3.cloned.1.call-done
  289.3 0.0 copy-done.1
  289.3 5.4 %fusion.22 = f32[480,768]{1,0:T(8,128)} fusion(bf16[480,2560]{1,0:T(8,128)(2,1)S(1)} %copy-done.1, bf16[2560,768]{1,0:T(8,128)(2,1)} %all-gather.3.cloned.1.call-done), kind=kOutput, calls=%fused_computation.58 | convolution fusion | flops 1887436800 | bytes 7864320 | tf_op jit(solution)/shard_map/dot_general | solution.py:52
  294.7 0.0 all-gather.5.cloned.1.call-done
  294.7 10.6 %convolution_convert_fusion = bf16[768,2560]{1,0:T(8,128)(2,1)} fusion(bf16[480,2560]{1,0:T(8,128)(2,1)} %reshape.172, f32[480,768]{1,0:T(8,128)} %fusion.22, bf16[480,2560]{1,0:T(8,128)(2,1)S(1)} %copy-done.1, bf16[2560,768]{1,0:T(8,128)(2,1)} %all-gather.5.cloned.1.call-done), kind=kOutput, calls=%fused_computation | convolution fusion | flops 3779051520 | bytes 14254080 | tf_op jit(solution)/shard_map/dot_general | solution.py:64
  305.3 0.0 reduce-scatter.2.cloned.1.call-update
  305.3 20.6 %reduce-scatter.2.cloned.1.call-done = bf16[384,2560]{1,0:T(8,128)(2,1)} async-done(((bf16[768,2560]{1,0:T(8,128)(2,1)}), bf16[384,2560]{1,0:T(8,128)(2,1)}) %reduce-scatter.2.cloned.1.call-update) | async-done | bytes 1966096 | tf_op jit(solution)/shard_map/reduce_scatter | solution.py:63
  326.0 4.0 %bitcast_convert_fusion = f32[1,384,2560]{2,1,0:T(8,128)} fusion(bf16[384,2560]{1,0:T(8,128)(2,1)} %reduce-scatter.2.cloned.1.call-done), kind=kLoop, calls=%fused_computation.3 | loop fusion | flops 983040 | bytes 5898240 | tf_op jit(solution)/shard_map/broadcast_in_dim | solution.py:71
  (6 shorter events, 0.1 us)
Async XLA Ops:
  6.5 13.8 %copy-start = (bf16[64,2560]{1,0:T(8,128)(2,1)S(1)}, bf16[64,2560]{1,0:T(8,128)(2,1)}, u32[]{:S(2)}) copy-start(bf16[64,2560]{1,0:T(8,128)(2,1)} %param.7) | copy-start | bytes 983044
  6.5 118.2 %collective-permute-start = (bf16[1280,768]{1,0:T(8,128)(2,1)}, bf16[1280,768]{1,0:T(8,128)(2,1)}, u32[]{:S(2)}, u32[]{:S(2)}) collective-permute-start(bf16[1280,768]{1,0:T(8,128)(2,1)} %bitcast.46), channel_id=1, source_target_pairs={{0,8},{1,9},{2,10},{3,11},{4,12},{5,13},{6,14},{7,15},{8,0},{9,1},... | collective-permute-start | bytes 5898248 | tf_op jit(solution)/shard_map/ppermute | solution.py:8
  23.4 163.1 %all-to-all-start = ((bf16[16,30,2560]{2,1,0:T(8,128)(2,1)}), bf16[16,30,2560]{2,1,0:T(8,128)(2,1)S(1)}, u32[]{:S(2)}, u32[]{:S(2)}) async-start(bf16[16,30,2560]{2,1,0:T(8,128)(2,1)} %reshape.169), calls=%async_computation | async-start | bytes 5242880 | tf_op jit(solution)/shard_map/all_to_all | solution.py:42
  28.3 261.0 %all-gather.3.cloned.1.call-start = ((), (), s32[]{:S(2)}) async-start(), calls=%async_computation.3 | async-start | bytes 5898240 | tf_op jit(solution)/shard_map/all_gather | solution.py:54
  124.8 3.8 %copy-start.3 = (s32[64,6]{0,1:T(8,128)S(1)}, s32[64,6]{0,1:T(8,128)}, u32[]{:S(2)}) copy-start(s32[64,6]{0,1:T(8,128)} %param.12) | copy-start | bytes 4612
  124.8 4.0 %copy-start.2 = (bf16[64,2560]{1,0:T(8,128)(2,1)S(1)}, bf16[64,2560]{1,0:T(8,128)(2,1)}, u32[]{:S(2)}) copy-start(bf16[64,2560]{1,0:T(8,128)(2,1)} %param.8) | copy-start | bytes 983044
  128.4 136.8 %collective-permute-start.1 = (bf16[1280,768]{1,0:T(8,128)(2,1)}, bf16[1280,768]{1,0:T(8,128)(2,1)}, u32[]{:S(2)}, u32[]{:S(2)}) collective-permute-start(bf16[1280,768]{1,0:T(8,128)(2,1)} %bitcast.47), channel_id=1, source_target_pairs={{0,8},{1,9},{2,10},{3,11},{4,12},{5,13},{6,14},{7,15},{8,0},{9,1},... | collective-permute-start | bytes 5898248 | tf_op jit(solution)/shard_map/ppermute | solution.py:8
  186.6 98.5 %all-to-all-start.1 = ((bf16[16,30,2560]{2,1,0:T(8,128)(2,1)}), bf16[16,30,2560]{2,1,0:T(8,128)(2,1)}, u32[]{:S(2)}, u32[]{:S(2)}) async-start(bf16[16,30,2560]{2,1,0:T(8,128)(2,1)} %reshape.171), calls=%async_computation.1 | async-start | bytes 5242880 | tf_op jit(solution)/shard_map/all_to_all | solution.py:43
  200.9 93.8 %all-gather.5.cloned.1.call-start = ((), (), s32[]{:S(2)}) async-start(), calls=%async_computation.4 | async-start | bytes 5898240 | tf_op jit(solution)/shard_map/all_gather | solution.py:59
  268.9 57.0 %reduce-scatter.2.cloned.1.call-start = ((), (), s32[]{:S(2)}) async-start(), calls=%async_computation.5 | async-start | bytes 5898240 | tf_op jit(solution)/shard_map/reduce_scatter | solution.py:63
  271.3 18.0 %copy-start.1 = (bf16[480,2560]{1,0:T(8,128)(2,1)S(1)}, bf16[480,2560]{1,0:T(8,128)(2,1)}, u32[]{:S(2)}) copy-start(bf16[480,2560]{1,0:T(8,128)(2,1)} %reshape.170) | copy-start | bytes 7372804
Sparse Core Ops, SparseCore 0:
  128.6 13.1 all-gather.2
  269.1 13.1 all-gather.4
  305.4 20.4 reduce-scatter.1
where the time goes:
time: 337 us; the launch traced here: 336 us
  waiting for transfers between devices  246 us (73%)
  starting transfers between devices  23.4 us (7%)
  matrix products  19.1 us (6%)
  other arithmetic  17.6 us (5%)
  local copies, waits for them, and re-layouts  16.5 us (5%)
  between operations  13.9 us (4%)
    ppermute x2, waiting for transfers between devices, from_partner(): lax.ppermute(value, axis, [(i, i ^ 1 << apart) for i in range(lax.axis_si...  160 us
    all_to_all x1, waiting for transfers between devices, shards(): lax.all_to_all(send_rows, 'expert', split_axis=0, concat_axis=0, tiled=True)  51.3 us
    reduce_scatter x1, waiting for transfers between devices, shards(): lax.psum_scatter(lax.dot_general(hidden, recv_grads, (((0,), (0,)), ((),...  20.6 us
    all_to_all x1, starting transfers between devices, shards(): lax.all_to_all(send_grads, 'expert', split_axis=0, concat_axis=0, tiled=T...  14.4 us
    all_to_all x1, waiting for transfers between devices, shards(): lax.all_to_all(send_grads, 'expert', split_axis=0, concat_axis=0, tiled=T...  13.8 us
    dot_general x1, matrix products, shards(): lax.dot_general(hidden, recv_grads, (((0,), (0,)), ((), ())), preferred_e...  10.6 us
  transfers between devices with their start and end apart: 7, of which 5 were waited for; matrix products, arithmetic and copies ran while one was open for 12% of the time, Pallas kernels for 0%

commit v1 on v0

v1 whole, which is shorter than its diff:
```python
import jax
import jax.numpy as jnp
from jax import lax
from jax.sharding import PartitionSpec as P


def from_partner(value, axis, apart):
    return lax.ppermute(value, axis, [(i, i ^ 1 << apart) for i in range(lax.axis_size(axis))])


def shards(tokens, cotangent, w_gate, w_up, expert_ids, gate_num, swap_flags):
    expert_count = lax.axis_size("expert")
    half_count = expert_count // 2
    swap_bit = expert_count.bit_length() - 2
    my_index = lax.axis_index("expert")
    tok_count, top_count = expert_ids.shape
    capacity = 5 * tok_count * top_count // (4 * expert_count)
    width = tokens.shape[1]
    my_flag = swap_flags[my_index % half_count] == 1
    flat_ids = expert_ids.reshape(-1)
    columns = jnp.arange(expert_count, dtype=jnp.int32)
    one_hot = (flat_ids[:, None] == columns[None, :]).astype(jnp.int32)
    ranking = jnp.sum((jnp.cumsum(one_hot, axis=0) - one_hot) * one_hot, axis=1)
    slot_ids = jnp.arange(expert_count * capacity, dtype=jnp.int32)

    def picked_by(destination):
        slot = destination * capacity + ranking
        return (slot_ids[:, None] == slot[None, :]).reshape(
            expert_count * capacity, tok_count, top_count
        )

    token_map = jnp.sum(picked_by(flat_ids).astype(jnp.int32), axis=2).astype(jnp.bfloat16)
    holder = jnp.where(
        swap_flags[flat_ids % half_count] == 1, (flat_ids + half_count) % expert_count, flat_ids
    )
    fractions = gate_num.astype(jnp.float32) / 64.0
    weight_map = jnp.sum(jnp.where(picked_by(holder), fractions[None], 0.0), axis=2).astype(jnp.bfloat16)
    send_rows = jnp.dot(token_map, tokens, preferred_element_type=jnp.float32).astype(jnp.bfloat16)
    send_grads = jnp.dot(weight_map, cotangent, preferred_element_type=jnp.float32).astype(
        jnp.bfloat16
    )

    def exchange(value):
        value = value.reshape(expert_count, capacity, width)
        value = lax.all_to_all(value, "expert", split_axis=0, concat_axis=0, tiled=True)
        return value.reshape(expert_count * capacity, width)

    gate_rows = lax.all_gather(w_gate[0], "dp", axis=0, tiled=True)
    up_rows = lax.all_gather(w_up[0], "dp", axis=0, tiled=True)
    recv_rows = exchange(send_rows)
    gate_sum = jnp.dot(recv_rows, gate_rows, preferred_element_type=jnp.float32)
    up_sum = jnp.dot(recv_rows, up_rows, preferred_element_type=jnp.float32)
    hidden = (jax.nn.silu(gate_sum) * up_sum).astype(jnp.bfloat16)
    other = from_partner(hidden, "expert", swap_bit)
    recv_grads = exchange(send_grads)
    hidden = jnp.where(my_flag, other, hidden)
    grads = lax.psum_scatter(
        lax.dot_general(
            hidden, recv_grads, (((0,), (0,)), ((), ())), preferred_element_type=jnp.float32
        ).astype(jnp.bfloat16),
        "dp",
        scatter_dimension=0,
        tiled=True,
    ).astype(jnp.float32)
    return grads[None]


def solution(mesh):
    in_specs = (
        P(("dp", "expert"), None),
        P(("dp", "expert"), None),
        P("expert", "dp", None),
        P("expert", "dp", None),
        P(("dp", "expert"), None),
        P(("dp", "expert"), None),
        P(),
    )
    out_specs = P("expert", "dp", None)
    return jax.shard_map(shards, mesh=mesh, in_specs=in_specs, out_specs=out_specs, check_vma=False)
```

time: 337 us -> 211 us (0.63)
  waiting for transfers between devices: 246 us -> 128 us
  other arithmetic: 17.6 us -> 11 us
    ppermute x2 -> x1, waiting for transfers between devices: 160 us -> 20.4 us  [from_partner(): lax.ppermute(value, axis, [(i, i ^ 1 << apart) for i in range(lax.axis_si...]
    all_to_all x2, waiting for transfers between devices: 65.1 us -> 94.9 us  [exchange(): lax.all_to_all(value, 'expert', split_axis=0, concat_axis=0, tiled=True)]
    reduce_scatter x1, waiting for transfers between devices: 20.6 us -> 11 us  [shards(): lax.psum_scatter(lax.dot_general(hidden, recv_grads, (((0,), (0,)), ((),...]
    select_n x4 -> x0, other arithmetic: 7.86 us -> none  [the longest x1 3.65 us: shards(): gate_rows = jnp.where(my_flag, other_gate, gate_rows)]
    dot_general x1 -> x2, matrix products: 5.36 us -> 10.9 us  [the longest x1 6.21 us: shards(): gate_sum = jnp.dot(recv_rows, gate_rows, preferred_element_type=jnp.float32)]
    dot_general x1, matrix products: 10.6 us -> 5.28 us  [shards(): lax.dot_general(hidden, recv_grads, (((0,), (0,)), ((), ())), preferred_e...]
  transfers between devices with their start and end apart: 7 -> 6, of which waited for: 5 -> 4; matrix products, arithmetic and copies ran while one was open for 12% -> 17% of each run, Pallas kernels for 0% -> 0%
where the time goes in v1:
time: 211 us
  waiting for transfers between devices  128 us (61%)
  starting transfers between devices  23.7 us (11%)
  matrix products  19.3 us (9%)
  local copies, waits for them, and re-layouts  15.2 us (7%)
  between operations  13.9 us (7%)
  other arithmetic  11 us (5%)
    all_to_all x2, waiting for transfers between devices, exchange(): lax.all_to_all(value, 'expert', split_axis=0, concat_axis=0, tiled=True)  94.9 us
    all_to_all x2, starting transfers between devices, exchange(): lax.all_to_all(value, 'expert', split_axis=0, concat_axis=0, tiled=True)  20.8 us
    ppermute x1, waiting for transfers between devices, from_partner(): lax.ppermute(value, axis, [(i, i ^ 1 << apart) for i in range(lax.axis_si...  20.4 us
    reduce_scatter x1, waiting for transfers between devices, shards(): lax.psum_scatter(lax.dot_general(hidden, recv_grads, (((0,), (0,)), ((),...  11 us
    reshape x2, local copies, waits for them, and re-layouts, exchange(): value = value.reshape(expert_count, capacity, width)  6.57 us
    dot_general x1, matrix products, shards(): gate_sum = jnp.dot(recv_rows, gate_rows, preferred_element_type=jnp.float32)  6.21 us
    dot_general x1, matrix products, shards(): lax.dot_general(hidden, recv_grads, (((0,), (0,)), ((), ())), preferred_e...  5.28 us
    reshape x2, local copies, waits for them, and re-layouts, exchange(): return value.reshape(expert_count * capacity, width)  5.04 us
  transfers between devices with their start and end apart: 6, of which 4 were waited for; matrix products, arithmetic and copies ran while one was open for 17% of the time, Pallas kernels for 0%

profile of v1, /device:TPU:0, one launch (start us, length us, event | category | flops | bytes accessed | tf_op | source)
XLA Modules:
  0.0 210.9 jit_solution(16730330350819116215)
XLA Ops:
  6.5 0.0 copy-start
  6.5 0.0 all-gather.5.cloned.1.call-start
  6.5 0.7 all-gather.5.cloned.1.call-update
  7.3 0.8 copy.30
  8.1 0.1 reshape.154
  8.2 0.1 eq.84
  8.3 0.1 eq.80
  8.5 1.7 fusion.21
  10.2 4.3 %fusion.19 = (s32[384]{0:T(512)S(1)}, s32[384,1]{0,1:T(1,128)S(1)}) fusion(s32[]{:T(128)} %bitcast.5, s32[]{:T(128)} %bitcast.6, s32[]{:T(128)} %bitcast.7, s32[]{:T(128)} %bitcast.8, s32[]{:T(128)} %bitcast.9, s32[]{:T(128)} %bitcast.11, s32[]{:T(128)} %bitcast.10, s32[384,1]{0,1:T(1,128)S(1)} %reshape.154), kind=kLoop, calls=%fused_computation.48 | loop fusion | flops 9984 | bytes 4636 | tf_op jit(solution)/shard_map/gather | solution.py:34
  14.5 0.7 select_compare_fusion
  15.2 0.2 eq.93
  15.4 0.1 copy.35
  15.5 0.9 reduce-window.6
  16.3 0.2 slice_reduce_fusion
  16.6 0.1 fusion.12
  16.7 0.1 reduce_sum.30
  16.8 0.1 copy.33
  16.9 0.7 multiply_add_fusion
  17.6 0.1 convert_reduce_fusion
  17.8 0.0 copy-done
  17.8 0.8 convolution_convert_fusion.2
  18.6 2.4 %reshape.152 = bf16[16,30,2560]{2,1,0:T(8,128)(2,1)} reshape(bf16[480,2560]{1,0:T(8,128)(2,1)S(1)} %convolution_convert_fusion.2) | data formatting | bytes 4915200 | tf_op jit(solution)/shard_map/reshape | solution.py:44
  21.0 0.0 copy-start.3
  21.0 0.0 copy-start.2
  21.0 8.4 %all-to-all-start = ((bf16[16,30,2560]{2,1,0:T(8,128)(2,1)}), bf16[16,30,2560]{2,1,0:T(8,128)(2,1)S(1)}, u32[]{:S(2)}, u32[]{:S(2)}) async-start(bf16[16,30,2560]{2,1,0:T(8,128)(2,1)} %reshape.152), calls=%async_computation | async-start | bytes 5242880 | tf_op jit(solution)/shard_map/all_to_all | solution.py:45
  29.4 0.0 all-gather.7.cloned.1.call-start
  29.5 0.7 all-gather.7.cloned.1.call-update
  30.2 0.0 copy-done.3
  30.2 0.2 select_reduce_fusion
  30.4 0.0 copy-done.2
  30.4 2.3 %convolution_convert_fusion.1 = bf16[480,2560]{1,0:T(8,128)(2,1)} fusion(bf16[64,2560]{1,0:T(8,128)(2,1)S(1)} %copy-done.2, bf16[480,64]{0,1:T(8,128)(2,1)S(1)} %select_reduce_fusion), kind=kOutput, calls=%fused_computation.1 | convolution fusion | flops 158515200 | bytes 2846720 | tf_op jit(solution)/shard_map/dot_general | solution.py:39
  32.7 4.2 %reshape.155 = bf16[16,30,2560]{2,1,0:T(8,128)(2,1)} reshape(bf16[480,2560]{1,0:T(8,128)(2,1)} %convolution_convert_fusion.1) | data formatting | bytes 4915200 | tf_op jit(solution)/shard_map/reshape | solution.py:44
  36.9 44.6 %all-to-all-done = bf16[16,30,2560]{2,1,0:T(8,128)(2,1)S(1)} async-done(((bf16[16,30,2560]{2,1,0:T(8,128)(2,1)}), bf16[16,30,2560]{2,1,0:T(8,128)(2,1)S(1)}, u32[]{:S(2)}, u32[]{:S(2)}) %all-to-all-start) | async-done | bytes 2457632 | tf_op jit(solution)/shard_map/all_to_all | solution.py:45
  81.4 12.4 %all-to-all-start.1 = ((bf16[16,30,2560]{2,1,0:T(8,128)(2,1)}), bf16[16,30,2560]{2,1,0:T(8,128)(2,1)}, u32[]{:S(2)}, u32[]{:S(2)}) async-start(bf16[16,30,2560]{2,1,0:T(8,128)(2,1)} %reshape.155), calls=%async_computation.1 | async-start | bytes 5242880 | tf_op jit(solution)/shard_map/all_to_all | solution.py:45
  93.8 0.0 reduce-scatter.2.cloned.1.call-start
  93.9 2.3 %reshape.153 = bf16[480,2560]{1,0:T(8,128)(2,1)} reshape(bf16[16,30,2560]{2,1,0:T(8,128)(2,1)S(1)} %all-to-all-done) | data formatting | bytes 4915200 | tf_op jit(solution)/shard_map/reshape | solution.py:46
  96.1 0.0 copy-start.1
  96.1 0.0 all-gather.5.cloned.1.call-done
  96.1 6.2 %fusion.2 = f32[480,768]{1,0:T(8,128)} fusion(bf16[480,2560]{1,0:T(8,128)(2,1)} %reshape.153, bf16[1,2560,768]{2,1,0:T(8,128)(2,1)} %all-gather.5.cloned.1.call-done), kind=kOutput, calls=%fused_computation.5 | convolution fusion | flops 1887436800 | bytes 7864320 | tf_op jit(solution)/shard_map/dot_general | solution.py:51
  102.3 0.0 all-gather.7.cloned.1.call-done
  102.3 0.0 copy-done.1
  102.3 4.7 %multiply_convert_fusion = bf16[480,768]{1,0:T(8,128)(2,1)S(1)} fusion(f32[480,768]{1,0:T(8,128)} %fusion.2, bf16[480,2560]{1,0:T(8,128)(2,1)S(1)} %copy-done.1, bf16[1,2560,768]{2,1,0:T(8,128)(2,1)} %all-gather.7.cloned.1.call-done), kind=kOutput, calls=%fused_computation.8 | convolution fusion | flops 1889648640 | bytes 8601600 | tf_op jit(solution)/shard_map/dot_general | solution.py:52
  107.0 2.8 %collective-permute-start = (bf16[480,768]{1,0:T(8,128)(2,1)S(1)}, bf16[480,768]{1,0:T(8,128)(2,1)}, u32[]{:S(2)}, u32[]{:S(2)}) collective-permute-start(bf16[480,768]{1,0:T(8,128)(2,1)S(1)} %multiply_convert_fusion), channel_id=1, source_target_pairs={{0,8},{1,9},{2,10},{3,11},{4,12},{5,13},{6,14},{7,15},{8,0},{9,1},... | collective-permute-start | bytes 2211848 | tf_op jit(solution)/shard_map/ppermute | solution.py:8
  110.6 50.3 %all-to-all-done.1 = bf16[16,30,2560]{2,1,0:T(8,128)(2,1)} async-done(((bf16[16,30,2560]{2,1,0:T(8,128)(2,1)}), bf16[16,30,2560]{2,1,0:T(8,128)(2,1)}, u32[]{:S(2)}, u32[]{:S(2)}) %all-to-all-start.1) | async-done | bytes 2457632 | tf_op jit(solution)/shard_map/all_to_all | solution.py:45
  160.9 2.8 %reshape.156 = bf16[480,2560]{1,0:T(8,128)(2,1)S(1)} reshape(bf16[16,30,2560]{2,1,0:T(8,128)(2,1)} %all-to-all-done.1) | data formatting | bytes 4915200 | tf_op jit(solution)/shard_map/reshape | solution.py:46
  163.7 20.4 %collective-permute-done = bf16[480,768]{1,0:T(8,128)(2,1)} collective-permute-done((bf16[480,768]{1,0:T(8,128)(2,1)S(1)}, bf16[480,768]{1,0:T(8,128)(2,1)}, u32[]{:S(2)}, u32[]{:S(2)}) %collective-permute-start) | collective-permute-done | bytes 737312 | tf_op jit(solution)/shard_map/ppermute | solution.py:8
  184.1 5.3 %convolution_convert_fusion = bf16[768,2560]{1,0:T(8,128)(2,1)} fusion(bf16[480,2560]{1,0:T(8,128)(2,1)S(1)} %reshape.156, bf16[480,768]{1,0:T(8,128)(2,1)} %collective-permute-done, bf16[480,768]{1,0:T(8,128)(2,1)S(1)} %multiply_convert_fusion, pred[]{:T(512)} %bitcast), kind=kOutput, calls=%fused_computation | convolution fusion | flops 1889771520 | bytes 7864321 | tf_op jit(solution)/shard_map/dot_general | solution.py:58
  189.4 0.0 reduce-scatter.2.cloned.1.call-update
  189.4 11.0 %reduce-scatter.2.cloned.1.call-done = bf16[384,2560]{1,0:T(8,128)(2,1)} async-done(((bf16[768,2560]{1,0:T(8,128)(2,1)}), bf16[384,2560]{1,0:T(8,128)(2,1)}) %reduce-scatter.2.cloned.1.call-update) | async-done | bytes 1966096 | tf_op jit(solution)/shard_map/reduce_scatter | solution.py:57
  200.4 4.0 %bitcast_convert_fusion = f32[1,384,2560]{2,1,0:T(8,128)} fusion(bf16[384,2560]{1,0:T(8,128)(2,1)} %reduce-scatter.2.cloned.1.call-done), kind=kLoop, calls=%fused_computation.7 | loop fusion | flops 983040 | bytes 5898240 | tf_op jit(solution)/shard_map/broadcast_in_dim | solution.py:65
  (4 shorter events, 0.1 us)
Async XLA Ops:
  6.5 11.2 %copy-start = (bf16[64,2560]{1,0:T(8,128)(2,1)S(1)}, bf16[64,2560]{1,0:T(8,128)(2,1)}, u32[]{:S(2)}) copy-start(bf16[64,2560]{1,0:T(8,128)(2,1)} %param.7) | copy-start | bytes 983044
  6.5 89.6 %all-gather.5.cloned.1.call-start = ((), (), s32[]{:S(2)}) async-start(), calls=%async_computation.4 | async-start | bytes 5898240 | tf_op jit(solution)/shard_map/all_gather | solution.py:48
  21.0 9.2 %copy-start.3 = (s32[64,6]{0,1:T(8,128)S(1)}, s32[64,6]{0,1:T(8,128)}, u32[]{:S(2)}) copy-start(s32[64,6]{0,1:T(8,128)} %param.12) | copy-start | bytes 4612
  21.0 9.4 %copy-start.2 = (bf16[64,2560]{1,0:T(8,128)(2,1)S(1)}, bf16[64,2560]{1,0:T(8,128)(2,1)}, u32[]{:S(2)}) copy-start(bf16[64,2560]{1,0:T(8,128)(2,1)} %param.8) | copy-start | bytes 983044
  21.0 60.5 %all-to-all-start = ((bf16[16,30,2560]{2,1,0:T(8,128)(2,1)}), bf16[16,30,2560]{2,1,0:T(8,128)(2,1)S(1)}, u32[]{:S(2)}, u32[]{:S(2)}) async-start(bf16[16,30,2560]{2,1,0:T(8,128)(2,1)} %reshape.152), calls=%async_computation | async-start | bytes 5242880 | tf_op jit(solution)/shard_map/all_to_all | solution.py:45
  29.4 72.9 %all-gather.7.cloned.1.call-start = ((), (), s32[]{:S(2)}) async-start(), calls=%async_computation.5 | async-start | bytes 5898240 | tf_op jit(solution)/shard_map/all_gather | solution.py:49
  81.4 79.4 %all-to-all-start.1 = ((bf16[16,30,2560]{2,1,0:T(8,128)(2,1)}), bf16[16,30,2560]{2,1,0:T(8,128)(2,1)}, u32[]{:S(2)}, u32[]{:S(2)}) async-start(bf16[16,30,2560]{2,1,0:T(8,128)(2,1)} %reshape.155), calls=%async_computation.1 | async-start | bytes 5242880 | tf_op jit(solution)/shard_map/all_to_all | solution.py:45
  93.8 106.6 %reduce-scatter.2.cloned.1.call-start = ((), (), s32[]{:S(2)}) async-start(), calls=%async_computation.3 | async-start | bytes 5898240 | tf_op jit(solution)/shard_map/reduce_scatter | solution.py:57
  96.1 6.2 %copy-start.1 = (bf16[480,2560]{1,0:T(8,128)(2,1)S(1)}, bf16[480,2560]{1,0:T(8,128)(2,1)}, u32[]{:S(2)}) copy-start(bf16[480,2560]{1,0:T(8,128)(2,1)} %reshape.153) | copy-start | bytes 7372804
  107.0 77.1 %collective-permute-start = (bf16[480,768]{1,0:T(8,128)(2,1)S(1)}, bf16[480,768]{1,0:T(8,128)(2,1)}, u32[]{:S(2)}, u32[]{:S(2)}) collective-permute-start(bf16[480,768]{1,0:T(8,128)(2,1)S(1)} %multiply_convert_fusion), channel_id=1, source_target_pairs={{0,8},{1,9},{2,10},{3,11},{4,12},{5,13},{6,14},{7,15},{8,0},{9,1},... | collective-permute-start | bytes 2211848 | tf_op jit(solution)/shard_map/ppermute | solution.py:8
Sparse Core Ops, SparseCore 0:
  8.9 15.9 all-gather.4
  31.8 14.5 all-gather.6
  189.5 10.8 reduce-scatter.1

commit v2 on v1

--- a/solution.py
+++ b/solution.py
@@ -1,6 +1,8 @@
 import jax
 import jax.numpy as jnp
 from jax import lax
+from jax.experimental import pallas as pl
+from jax.experimental.pallas import tpu as pltpu
 from jax.sharding import PartitionSpec as P
 
 
@@ -65,7 +67,293 @@
     return grads[None]
 
 
+ZS, LANES, SLOTS, TILES = 4, 128, 32, 5
+
+
+def kernel(flags_ref, ids_ref, num_ref, tok_hbm, cot_hbm, wg_hbm, wu_hbm, out_ref,
+           tok, cot, wg, wu, picked, hid, hid_other, hid_t, scaled, part, part_other,
+           local_sem, z_send, z_recv, c_send, c_recv, d_send, d_recv,
+           w_send, w_recv, h_send, h_recv, p_send, p_recv):
+    rows, width = tok_hbm.shape
+    count = ids_ref.shape[1]
+    half, ff = wg_hbm.shape
+    mine = ff // 2
+    experts = 4 * ZS
+    dp, me = lax.axis_index("dp"), lax.axis_index("expert")
+    x, y, z = me % 2, (me // 2) % 2, me // 4
+    to_x, to_y = (dp, me + 1 - 2 * x), (dp, me + 2 - 4 * y)
+    up, down = (dp, me + 4), (dp, me - 4)
+    pair = (dp, (me + 8) % experts)
+    twin = (1 - dp, me)
+    col, x_col, y_col = me % 4, me % 4 + 1 - 2 * x, me % 4 + 2 - 4 * y
+    d_col = 3 - col
+
+    barrier = pltpu.get_barrier_semaphore()
+
+    def greet(device):
+        pl.semaphore_signal(barrier, inc=1, device_id=device, device_id_type=pl.DeviceIdType.MESH)
+
+    for device in (to_x, to_y, pair, twin):
+        greet(device)
+    pl.when(z < ZS - 1)(lambda: greet(up))
+    pl.when(z > 0)(lambda: greet(down))
+
+    def shard(column, s):
+        return pl.ds(pl.multiple_of((column * ZS + z + s) * rows, rows), rows)
+
+    def remote(ref, send, recv, device, target=None):
+        return pltpu.make_async_remote_copy(
+            src_ref=ref, dst_ref=ref if target is None else target, send_sem=send, recv_sem=recv,
+            device_id=device, device_id_type=pl.DeviceIdType.MESH)
+
+    own = shard(col, 0)
+    loads = [
+        pltpu.make_async_copy(tok_hbm, tok.at[own, pl.ds(0, width)], local_sem.at[0]),
+        pltpu.make_async_copy(cot_hbm, cot.at[own], local_sem.at[1]),
+        pltpu.make_async_copy(wg_hbm, wg.at[dp], local_sem.at[2]),
+        pltpu.make_async_copy(wu_hbm, wu.at[dp], local_sem.at[3]),
+    ]
+    for load in loads:
+        load.start()
+
+    lanes = lax.broadcasted_iota(jnp.int32, (rows, LANES), 1)
+    fractions = num_ref[...].astype(jnp.float32) / 64.0
+    table = jnp.zeros((rows, LANES), jnp.float32)
+    for k in range(count):
+        table = jnp.where(lanes == ids_ref[:, k:k + 1], fractions[:, k:k + 1], table)
+    tok[own, pl.ds(width, LANES)] = table.astype(jnp.bfloat16)
+
+    inner = (z > 0) & (z < ZS - 1)
+    pl.when(inner)(lambda: pl.semaphore_wait(barrier, 6))
+    pl.when(jnp.logical_not(inner))(lambda: pl.semaphore_wait(barrier, 5))
+
+    arrays = (tok, cot)
+
+    def valid(s):
+        return z + s >= 0 if s < 0 else z + s < ZS
+
+    def z_copy(a, way, d, s):
+        return remote(arrays[a].at[shard(col, s)], z_send.at[a, way, d], z_recv.at[a, way, d],
+                      up if way == 0 else down)
+
+    def c_copy(a, way, s, column):
+        return remote(arrays[a].at[shard(column, s)], c_send.at[a, way, s + 3],
+                      c_recv.at[a, way, s + 3], to_x if way == 0 else to_y)
+
+    def d_copy(a, way, s, column):
+        start = (column * ZS + z + s) * rows + way * (rows // 2)
+        return remote(arrays[a].at[pl.ds(pl.multiple_of(start, rows // 2), rows // 2)],
+                      d_send.at[a, way, s + 3], d_recv.at[a, way, s + 3], to_x if way == 0 else to_y)
+
+    def z_sends(a, s, act):
+        if -3 < s <= 0:
+            pl.when(z < ZS - 1)(lambda: act(z_copy(a, 0, -s, s)))
+        if 0 <= s < 3:
+            pl.when(z > 0)(lambda: act(z_copy(a, 1, s, s)))
+
+    def begin(copy):
+        copy.start()
+
+    def own_plane(a, s):
+        c_copy(a, 0, s, col).start()
+        c_copy(a, 1, s, col).start()
+
+    def step_z(a, d):
+        for s in (-d, d):
+            @pl.when(valid(s))
+            def _(s=s):
+                z_copy(a, 0 if s < 0 else 1, d - 1, s).wait_recv()
+                z_sends(a, s, begin)
+                own_plane(a, s)
+
+    def step_plane(a, d):
+        for s in ((0,) if d == 0 else (-d, d)):
+            @pl.when(valid(s))
+            def _(s=s):
+                c_copy(a, 1, s, y_col).wait_recv()
+                d_copy(a, 0, s, y_col).start()
+                c_copy(a, 0, s, x_col).wait_recv()
+                d_copy(a, 1, s, x_col).start()
+
+    def step_diagonal(a):
+        for s in range(-3, 4):
+            @pl.when(valid(s))
+            def _(s=s):
+                d_copy(a, 0, s, d_col).wait_recv()
+                d_copy(a, 1, s, d_col).wait_recv()
+
+    chunk = ZS * rows
+    packed = ZS * SLOTS
+    flag = flags_ref[me % (experts // 2)]
+    held = jnp.where(flag == 1, (me + experts // 2) % experts, me)
+    t0 = lax.broadcasted_iota(jnp.int32, (chunk, chunk), 0)
+    t1 = lax.broadcasted_iota(jnp.int32, (chunk, chunk), 1)
+    earlier = jnp.where((t0 < t1) & (t0 // rows == t1 // rows), 1.0, 0.0).astype(jnp.bfloat16)
+
+    def chosen(column, expert, weighted):
+        r = pl.ds(pl.multiple_of(column * chunk, chunk), chunk)
+        one = jnp.where(lax.broadcasted_iota(jnp.int32, (16, LANES), 1) == expert, 1.0, 0.0)
+        weight = lax.dot_general(one.astype(jnp.bfloat16), tok[r, pl.ds(width, LANES)],
+                                 (((1,), (1,)), ((), ())), preferred_element_type=jnp.float32)
+        named = jnp.where(weight > 0.0, 1.0, 0.0)
+        rank = jnp.dot(named.astype(jnp.bfloat16), earlier, preferred_element_type=jnp.float32)
+        place = lax.broadcasted_iota(jnp.int32, (packed, chunk), 0)
+        token = lax.broadcasted_iota(jnp.int32, (packed, chunk), 1)
+        goal = (place % SLOTS).astype(jnp.float32)
+        hit = (goal == rank[0:1]) & (place // SLOTS == token // rows) & (weight[0:1] > 0.0)
+        value = weight[0:1] if weighted else named[0:1]
+        return jnp.where(hit, value, 0.0).astype(jnp.bfloat16)
+
+    def h_copy(k, column):
+        r = pl.ds(pl.multiple_of(column * packed, packed), packed)
+        return remote(hid.at[r], h_send.at[k], h_recv.at[k], pair, hid_other.at[r])
+
+    def hidden(k, column):
+        r = pl.ds(pl.multiple_of(column * chunk, chunk), chunk)
+        h = pl.ds(pl.multiple_of(column * packed, packed), packed)
+        take = chosen(column, me, False)
+
+        @pl.loop(0, width // 512)
+        def _(n):
+            c = pl.ds(pl.multiple_of(n * 512, 512), 512)
+            picked[:, c] = jnp.dot(take, tok[r, c], preferred_element_type=jnp.float32).astype(jnp.bfloat16)
+
+        @pl.loop(0, ff // 256)
+        def _(n):
+            c = pl.ds(pl.multiple_of(n * 256, 256), 256)
+            lo, hi = picked[:, 0:half], picked[:, half:2 * half]
+
+            def project(w):
+                return (jnp.dot(lo, w[0, :, c], preferred_element_type=jnp.float32)
+                        + jnp.dot(hi, w[1, :, c], preferred_element_type=jnp.float32))
+
+            gate, upper = project(wg), project(wu)
+            hid[h, c] = (gate / (1.0 + jnp.exp(-gate)) * upper).astype(jnp.bfloat16)
+
+        h_copy(k, column).start()
+
+    def scale(column):
+        r = pl.ds(pl.multiple_of(column * chunk, chunk), chunk)
+        h = pl.ds(pl.multiple_of(column * packed, packed), packed)
+        take = chosen(column, held, True)
+
+        @pl.loop(0, width // 512)
+        def _(n):
+            c = pl.ds(pl.multiple_of(n * 512, 512), 512)
+            scaled[h, c] = jnp.dot(take, cot[r, c], preferred_element_type=jnp.float32).astype(jnp.bfloat16)
+
+    loads[0].wait()
+    z_sends(0, 0, begin)
+    own_plane(0, 0)
+    weights = [remote(wg_hbm, w_send.at[0], w_recv.at[0], twin, wg.at[dp]),
+               remote(wu_hbm, w_send.at[1], w_recv.at[1], twin, wu.at[dp])]
+    for copy in weights:
+        copy.start()
+    loads[1].wait()
+    step_z(0, 1)
+    step_plane(0, 0)
+    step_z(0, 2)
+    z_sends(1, 0, begin)
+    step_plane(0, 1)
+    step_z(0, 3)
+    loads[2].wait()
+    loads[3].wait()
+    remote(wg.at[1 - dp], w_send.at[0], w_recv.at[0], twin).wait_recv()
+    remote(wu.at[1 - dp], w_send.at[1], w_recv.at[1], twin).wait_recv()
+    hidden(0, col)
+    step_plane(0, 2)
+    step_plane(0, 3)
+    own_plane(1, 0)
+    step_z(1, 1)
+    hidden(1, y_col)
+    hidden(2, x_col)
+    step_z(1, 2)
+    step_z(1, 3)
+    step_diagonal(0)
+    hidden(3, d_col)
+    for d in range(4):
+        step_plane(1, d)
+    for column in (col, y_col, x_col):
+        scale(column)
+    for k, column in enumerate((col, y_col, x_col, d_col)):
+        h_copy(k, column).wait_recv()
+    hid_t[...] = jnp.where(flag == 1, hid_other[...].astype(jnp.float32),
+                           hid[...].astype(jnp.float32)).T.astype(jnp.bfloat16)
+    step_diagonal(1)
+    scale(d_col)
+
+    tile = width // TILES
+
+    def product(core, n):
+        r = pl.ds(pl.multiple_of(core * mine, mine), mine)
+        c = pl.ds(pl.multiple_of(n * tile, tile), tile)
+        return jnp.dot(hid_t[r], scaled[:, c], preferred_element_type=jnp.float32).astype(jnp.bfloat16)
+
+    def p_copy(n):
+        return remote(part.at[n], p_send.at[n], p_recv.at[n], twin, part_other.at[n])
+
+    for n in range(TILES):
+        part[n] = product(1 - dp, n)
+        p_copy(n).start()
+    for n in range(TILES):
+        out_ref[:, n * tile:(n + 1) * tile] = product(dp, n).astype(jnp.float32)
+    for n in range(TILES):
+        p_copy(n).wait_recv()
+        out_ref[:, n * tile:(n + 1) * tile] += part_other[n].astype(jnp.float32)
+
+    for a in range(2):
+        for s in range(-3, 4):
+            @pl.when(valid(s))
+            def _(a=a, s=s):
+                z_sends(a, s, lambda copy: copy.wait_send())
+                for way in range(2):
+                    c_copy(a, way, s, col).wait_send()
+                d_copy(a, 0, s, y_col).wait_send()
+                d_copy(a, 1, s, x_col).wait_send()
+    for copy in weights:
+        copy.wait_send()
+    for k, column in enumerate((col, y_col, x_col, d_col)):
+        h_copy(k, column).wait_send()
+    for n in range(TILES):
+        p_copy(n).wait_send()
+
+
+def fused(tokens, cotangent, w_gate, w_up, expert_ids, gate_num, swap_flags):
+    rows, width = tokens.shape
+    _, half, ff = w_gate.shape
+    total, packed = 16 * rows, 16 * SLOTS
+    bf16, dma = jnp.bfloat16, pltpu.SemaphoreType.DMA
+    hbm, vmem = pl.BlockSpec(memory_space=pl.ANY), pl.BlockSpec(memory_space=pltpu.VMEM)
+    grads = pl.pallas_call(
+        kernel,
+        out_shape=jax.ShapeDtypeStruct((ff // 2, width), jnp.float32),
+        in_specs=[pl.BlockSpec(memory_space=pltpu.SMEM), vmem, vmem, hbm, hbm, hbm, hbm],
+        out_specs=vmem,
+        scratch_shapes=[
+            pltpu.VMEM((total, width + LANES), bf16),
+            pltpu.VMEM((total, width), bf16),
+            pltpu.VMEM((2, half, ff), bf16),
+            pltpu.VMEM((2, half, ff), bf16),
+            pltpu.VMEM((ZS * SLOTS, width), bf16),
+            pltpu.VMEM((packed, ff), bf16),
+            pltpu.VMEM((packed, ff), bf16),
+            pltpu.VMEM((ff, packed), bf16),
+            pltpu.VMEM((packed, width), bf16),
+            pltpu.VMEM((TILES, ff // 2, width // TILES), bf16),
+            pltpu.VMEM((TILES, ff // 2, width // TILES), bf16),
+            dma((4,)), dma((2, 2, 3)), dma((2, 2, 3)), dma((2, 2, 7)), dma((2, 2, 7)),
+            dma((2, 2, 7)), dma((2, 2, 7)), dma((2,)), dma((2,)), dma((4,)), dma((4,)),
+            dma((TILES,)), dma((TILES,)),
+        ],
+        compiler_params=pltpu.CompilerParams(
+            collective_id=0, has_side_effects=True, vmem_limit_bytes=52 * 1024 * 1024),
+        cost_estimate=pl.CostEstimate(flops=8 * 10**9, bytes_accessed=2 * 10**7, transcendentals=400000),
+    )(swap_flags, expert_ids, gate_num, tokens, cotangent, w_gate[0], w_up[0])
+    return grads[None]
+
+
 def solution(mesh):
+    small = mesh.shape["expert"] == 16 and mesh.shape["dp"] == 2
     in_specs = (
         P(("dp", "expert"), None),
         P(("dp", "expert"), None),
@@ -76,4 +364,4 @@
         P(),
     )
     out_specs = P("expert", "dp", None)
-    return jax.shard_map(shards, mesh=mesh, in_specs=in_specs, out_specs=out_specs, check_vma=False)
+    return jax.shard_map(fused if small else shards, mesh=mesh, in_specs=in_specs, out_specs=out_specs, check_vma=False)

time: 211 us -> 112 us (0.53)
  waiting for transfers between devices: 128 us -> 0 us
  Pallas kernels: 0 us -> 103 us
  starting transfers between devices: 23.7 us -> 0 us
  matrix products: 19.3 us -> 0 us
  between operations: 13.9 us -> 0.01 us
  other arithmetic: 11 us -> 0 us
  local copies, waits for them, and re-layouts: 15.2 us -> 8.44 us
    pallas_call x0 -> x1, Pallas kernels: none -> 103 us  [fused(): pl.pallas_call(kernel, out_shape=jax.ShapeDtypeStruct((ff // 2, width), j...]
    all_to_all x2 -> x0, waiting for transfers between devices: 94.9 us -> none  [exchange(): lax.all_to_all(value, 'expert', split_axis=0, concat_axis=0, tiled=True)]
    all_to_all x2 -> x0, starting transfers between devices: 20.8 us -> none  [exchange(): lax.all_to_all(value, 'expert', split_axis=0, concat_axis=0, tiled=True)]
    ppermute x1 -> x0, waiting for transfers between devices: 20.4 us -> none  [from_partner(): lax.ppermute(value, axis, [(i, i ^ 1 << apart) for i in range(lax.axis_si...]
    dot_general x5 -> x0, matrix products: 19.3 us -> none  [the longest x1 6.21 us: shards(): gate_sum = jnp.dot(recv_rows, gate_rows, preferred_element_type=jnp.float32)]
    reshape x5 -> x0, local copies, waits for them, and re-layouts: 11.7 us -> none  [the longest x2 6.57 us: exchange(): value = value.reshape(expert_count, capacity, width)]
    reduce_scatter x1 -> x0, waiting for transfers between devices: 11 us -> none  [shards(): lax.psum_scatter(lax.dot_general(hidden, recv_grads, (((0,), (0,)), ((),...]
    unnamed x9, local copies, waits for them, and re-layouts: 0.79 us -> 8.44 us
  transfers between devices with their start and end apart: 6 -> 0, of which waited for: 4 -> 0; matrix products, arithmetic and copies ran while one was open for 17% -> 0% of each run, Pallas kernels for 0% -> 0%
where the time goes in v2:
time: 112 us; the launch traced here: 111 us
  Pallas kernels  103 us (92%)
  local copies, waits for them, and re-layouts  8.44 us (8%)
    pallas_call x1, Pallas kernels, fused(): pl.pallas_call(kernel, out_shape=jax.ShapeDtypeStruct((ff // 2, width), j...  103 us
    unnamed x9, local copies, waits for them, and re-layouts  8.44 us

profile of v2, /device:TPU:0, one launch (start us, length us, event | category | flops | bytes accessed | tf_op | source)
XLA Modules:
  0.0 111.3 jit_solution(3724986564559504459)
XLA Ops:
  0.0 0.8 copy.8.ids_ref
  0.8 0.8 copy.9.num_ref
  1.6 0.0 copy-start
  1.6 1.0 copy-done
  2.5 0.0 copy-start.1
  2.5 1.0 copy-done.1
  3.5 0.0 copy-start.2
  3.5 0.7 copy-done.2
  4.2 102.9 %shard_map.73 = f32[384,2560]{1,0:T(8,128)} custom-call(s32[8]{0:T(128)S(1)} %copy-done.2, s32[64,6]{1,0:T(8,128)S(1)} %copy.8.ids_ref, s32[64,6]{1,0:T(8,128)S(1)} %copy.9.num_ref, bf16[64,2560]{1,0:T(8,128)(2,1)S(1)} %copy-done, bf16[64,2560]{1,0:T(8,128)(2,1)S(1)} %copy-done.1, bf16[1280,768]{1,0:T(8,128)(2,1)} %bitcast.4, bf16[1280,768]{1,0:T(8,128)(2,1)} %bitcast.5), custom_call_target="tpu_custom_call" | custom-call | flops 8000000000 | bytes 20000000 | tf_op jit(solution)/shard_map/pallas_call | solution.py:327
  107.0 4.3 %copy.11 = f32[1,384,2560]{2,1,0:T(8,128)} copy(f32[1,384,2560]{2,1,0:T(8,128)} %bitcast.3) | data formatting | bytes 7864320
Async XLA Ops:
  1.6 1.0 copy-start
  2.5 1.0 copy-start.1
  3.5 0.7 copy-start.2

commit v3 on v2

--- a/solution.py
+++ b/solution.py
@@ -70,12 +70,12 @@
 ZS, LANES, SLOTS, TILES = 4, 128, 32, 5
 
 
-def kernel(flags_ref, ids_ref, num_ref, tok_hbm, cot_hbm, wg_hbm, wu_hbm, out_ref,
-           tok, cot, wg, wu, picked, hid, hid_other, hid_t, scaled, part, part_other,
-           local_sem, z_send, z_recv, c_send, c_recv, d_send, d_recv,
+def kernel(flags_ref, ids_hbm, num_hbm, tok_hbm, cot_hbm, wg_hbm, wu_hbm, sum_hbm, other_hbm,
+           tok, cot, wg, wu, picked, hid, hid_other, hid_t, scaled, part, part_own, ids_ref, num_ref,
+           local_sem, z_send, z_recv, c_send, c_recv, d_send, d_recv, e_send, e_recv, o_sem,
            w_send, w_recv, h_send, h_recv, p_send, p_recv):
     rows, width = tok_hbm.shape
-    count = ids_ref.shape[1]
+    count = ids_hbm.shape[0]
     half, ff = wg_hbm.shape
     mine = ff // 2
     experts = 4 * ZS
@@ -113,15 +113,23 @@
         pltpu.make_async_copy(wg_hbm, wg.at[dp], local_sem.at[2]),
         pltpu.make_async_copy(wu_hbm, wu.at[dp], local_sem.at[3]),
     ]
-    for load in loads:
+    names = [pltpu.make_async_copy(ids_hbm, ids_ref, local_sem.at[4]),
+             pltpu.make_async_copy(num_hbm, num_ref, local_sem.at[5])]
+    for load in names + loads:
         load.start()
-
-    lanes = lax.broadcasted_iota(jnp.int32, (rows, LANES), 1)
+    for load in names:
+        load.wait()
+
+    lanes = lax.broadcasted_iota(jnp.int32, (LANES, rows), 0)
     fractions = num_ref[...].astype(jnp.float32) / 64.0
-    table = jnp.zeros((rows, LANES), jnp.float32)
+    table = jnp.zeros((LANES, rows), jnp.float32)
     for k in range(count):
-        table = jnp.where(lanes == ids_ref[:, k:k + 1], fractions[:, k:k + 1], table)
-    tok[own, pl.ds(width, LANES)] = table.astype(jnp.bfloat16)
+        table = jnp.where(lanes == ids_ref[k:k + 1, :], fractions[k:k + 1, :], table)
+    same = (lax.broadcasted_iota(jnp.int32, (rows, rows), 0)
+            == lax.broadcasted_iota(jnp.int32, (rows, rows), 1))
+    tok[own, pl.ds(width, LANES)] = lax.dot_general(
+        jnp.where(same, 1.0, 0.0).astype(jnp.bfloat16), table.astype(jnp.bfloat16),
+        (((1,), (1,)), ((), ())), preferred_element_type=jnp.float32).astype(jnp.bfloat16)
 
     inner = (z > 0) & (z < ZS - 1)
     pl.when(inner)(lambda: pl.semaphore_wait(barrier, 6))
@@ -141,15 +149,21 @@
                       c_recv.at[a, way, s + 3], to_x if way == 0 else to_y)
 
     def d_copy(a, way, s, column):
-        start = (column * ZS + z + s) * rows + way * (rows // 2)
+        size = rows // 2 if s == 0 else rows // 4
+        start = (column * ZS + z + s) * rows + way * size
+        return remote(arrays[a].at[pl.ds(pl.multiple_of(start, size), size)],
+                      d_send.at[a, way, s + 3], d_recv.at[a, way, s + 3], to_x if way == 0 else to_y)
+
+    def e_copy(a, way, d, s):
+        start = (d_col * ZS + z + s) * rows + rows // 2
         return remote(arrays[a].at[pl.ds(pl.multiple_of(start, rows // 2), rows // 2)],
-                      d_send.at[a, way, s + 3], d_recv.at[a, way, s + 3], to_x if way == 0 else to_y)
-
-    def z_sends(a, s, act):
+                      e_send.at[a, way, d], e_recv.at[a, way, d], up if way == 0 else down)
+
+    def z_sends(a, s, act, copy=z_copy):
         if -3 < s <= 0:
-            pl.when(z < ZS - 1)(lambda: act(z_copy(a, 0, -s, s)))
+            pl.when(z < ZS - 1)(lambda: act(copy(a, 0, -s, s)))
         if 0 <= s < 3:
-            pl.when(z > 0)(lambda: act(z_copy(a, 1, s, s)))
+            pl.when(z > 0)(lambda: act(copy(a, 1, s, s)))
 
     def begin(copy):
         copy.start()
@@ -175,12 +189,24 @@
                 c_copy(a, 0, s, x_col).wait_recv()
                 d_copy(a, 1, s, x_col).start()
 
+    def step_e(a, d):
+        if d == 0:
+            d_copy(a, 1, 0, d_col).wait_recv()
+            z_sends(a, 0, begin, e_copy)
+            return
+        for s in (-d, d):
+            @pl.when(valid(s))
+            def _(s=s):
+                e_copy(a, 0 if s < 0 else 1, d - 1, s).wait_recv()
+                z_sends(a, s, begin, e_copy)
+
     def step_diagonal(a):
         for s in range(-3, 4):
             @pl.when(valid(s))
             def _(s=s):
                 d_copy(a, 0, s, d_col).wait_recv()
-                d_copy(a, 1, s, d_col).wait_recv()
+                if s != 0:
+                    d_copy(a, 1, s, d_col).wait_recv()
 
     chunk = ZS * rows
     packed = ZS * SLOTS
@@ -253,17 +279,21 @@
     step_z(0, 1)
     step_plane(0, 0)
     step_z(0, 2)
+    step_e(0, 0)
     z_sends(1, 0, begin)
     step_plane(0, 1)
     step_z(0, 3)
+    step_e(0, 1)
     loads[2].wait()
     loads[3].wait()
     remote(wg.at[1 - dp], w_send.at[0], w_recv.at[0], twin).wait_recv()
     remote(wu.at[1 - dp], w_send.at[1], w_recv.at[1], twin).wait_recv()
     hidden(0, col)
+    step_e(0, 2)
     step_plane(0, 2)
+    own_plane(1, 0)
     step_plane(0, 3)
-    own_plane(1, 0)
+    step_e(0, 3)
     step_z(1, 1)
     hidden(1, y_col)
     hidden(2, x_col)
@@ -273,6 +303,7 @@
     hidden(3, d_col)
     for d in range(4):
         step_plane(1, d)
+        step_e(1, d)
     for column in (col, y_col, x_col):
         scale(column)
     for k, column in enumerate((col, y_col, x_col, d_col)):
@@ -290,22 +321,28 @@
         return jnp.dot(hid_t[r], scaled[:, c], preferred_element_type=jnp.float32).astype(jnp.bfloat16)
 
     def p_copy(n):
-        return remote(part.at[n], p_send.at[n], p_recv.at[n], twin, part_other.at[n])
+        return remote(part.at[n], p_send.at[n], p_recv.at[n], twin,
+                      other_hbm.at[:, pl.ds(n * tile, tile)])
+
+    def o_copy(n):
+        return pltpu.make_async_copy(part_own.at[n], sum_hbm.at[:, pl.ds(n * tile, tile)], o_sem.at[n])
 
     for n in range(TILES):
         part[n] = product(1 - dp, n)
         p_copy(n).start()
     for n in range(TILES):
-        out_ref[:, n * tile:(n + 1) * tile] = product(dp, n).astype(jnp.float32)
+        part_own[n] = product(dp, n)
+        o_copy(n).start()
     for n in range(TILES):
+        o_copy(n).wait()
         p_copy(n).wait_recv()
-        out_ref[:, n * tile:(n + 1) * tile] += part_other[n].astype(jnp.float32)
 
     for a in range(2):
         for s in range(-3, 4):
             @pl.when(valid(s))
             def _(a=a, s=s):
                 z_sends(a, s, lambda copy: copy.wait_send())
+                z_sends(a, s, lambda copy: copy.wait_send(), e_copy)
                 for way in range(2):
                     c_copy(a, way, s, col).wait_send()
                 d_copy(a, 0, s, y_col).wait_send()
@@ -323,12 +360,12 @@
     _, half, ff = w_gate.shape
     total, packed = 16 * rows, 16 * SLOTS
     bf16, dma = jnp.bfloat16, pltpu.SemaphoreType.DMA
-    hbm, vmem = pl.BlockSpec(memory_space=pl.ANY), pl.BlockSpec(memory_space=pltpu.VMEM)
-    grads = pl.pallas_call(
+    hbm = pl.BlockSpec(memory_space=pltpu.HBM)
+    term, other = pl.pallas_call(
         kernel,
-        out_shape=jax.ShapeDtypeStruct((ff // 2, width), jnp.float32),
-        in_specs=[pl.BlockSpec(memory_space=pltpu.SMEM), vmem, vmem, hbm, hbm, hbm, hbm],
-        out_specs=vmem,
+        out_shape=[jax.ShapeDtypeStruct((ff // 2, width), bf16)] * 2,
+        in_specs=[pl.BlockSpec(memory_space=pltpu.SMEM)] + [hbm] * 6,
+        out_specs=[hbm, hbm],
         scratch_shapes=[
             pltpu.VMEM((total, width + LANES), bf16),
             pltpu.VMEM((total, width), bf16),
@@ -341,15 +378,17 @@
             pltpu.VMEM((packed, width), bf16),
             pltpu.VMEM((TILES, ff // 2, width // TILES), bf16),
             pltpu.VMEM((TILES, ff // 2, width // TILES), bf16),
-            dma((4,)), dma((2, 2, 3)), dma((2, 2, 3)), dma((2, 2, 7)), dma((2, 2, 7)),
-            dma((2, 2, 7)), dma((2, 2, 7)), dma((2,)), dma((2,)), dma((4,)), dma((4,)),
+            pltpu.VMEM((expert_ids.shape[1], rows), jnp.int32),
+            pltpu.VMEM((expert_ids.shape[1], rows), jnp.int32),
+            dma((6,)), dma((2, 2, 3)), dma((2, 2, 3)), dma((2, 2, 7)), dma((2, 2, 7)),
+            dma((2, 2, 7)), dma((2, 2, 7)), dma((2, 2, 3)), dma((2, 2, 3)), dma((TILES,)), dma((2,)), dma((2,)), dma((4,)), dma((4,)),
             dma((TILES,)), dma((TILES,)),
         ],
         compiler_params=pltpu.CompilerParams(
-            collective_id=0, has_side_effects=True, vmem_limit_bytes=52 * 1024 * 1024),
+            collective_id=0, has_side_effects=True, vmem_limit_bytes=65408 * 1024),
         cost_estimate=pl.CostEstimate(flops=8 * 10**9, bytes_accessed=2 * 10**7, transcendentals=400000),
-    )(swap_flags, expert_ids, gate_num, tokens, cotangent, w_gate[0], w_up[0])
-    return grads[None]
+    )(swap_flags, expert_ids.T, gate_num.T, tokens, cotangent, w_gate[0], w_up[0])
+    return (term.astype(jnp.float32) + other.astype(jnp.float32))[None]
 
 
 def solution(mesh):

time: 112 us -> 129 us (1.15)
  Pallas kernels: 103 us -> 124 us
  local copies, waits for them, and re-layouts: 8.44 us -> 0 us
  other arithmetic: 0 us -> 4.63 us
    pallas_call x1, Pallas kernels: 103 us -> 124 us  [fused(): pl.pallas_call(kernel, out_shape=[jax.ShapeDtypeStruct((ff // 2, width),...]
    unnamed x9 -> x0, local copies, waits for them, and re-layouts: 8.44 us -> none
    broadcast_in_dim x0 -> x1, other arithmetic: none -> 4.63 us  [fused(): return (term.astype(jnp.float32) + other.astype(jnp.float32))[None]]
where the time goes in v3:
time: 129 us
  Pallas kernels  124 us (96%)
  other arithmetic  4.63 us (4%)
    pallas_call x1, Pallas kernels, fused(): pl.pallas_call(kernel, out_shape=[jax.ShapeDtypeStruct((ff // 2, width),...  124 us
    broadcast_in_dim x1, other arithmetic, fused(): return (term.astype(jnp.float32) + other.astype(jnp.float32))[None]  4.63 us

profile of v3, /device:TPU:0, one launch (start us, length us, event | category | flops | bytes accessed | tf_op | source)
XLA Modules:
  0.0 128.8 jit_solution(12149560092815288016)
XLA Ops:
  0.0 124.1 %shard_map.73 = (bf16[384,2560]{1,0:T(8,128)(2,1)}, bf16[384,2560]{1,0:T(8,128)(2,1)}) custom-call(s32[8]{0:T(128)} %flags_ref.1, s32[6,64]{1,0:T(8,128)} %bitcast.8, s32[6,64]{1,0:T(8,128)} %bitcast.9, bf16[64,2560]{1,0:T(8,128)(2,1)} %tok_hbm.1, bf16[64,2560]{1,0:T(8,128)(2,1)} %cot_hbm.1, bf16[1280,768]{1,0:T(8,128)(2,1)} %bitcast.6, ...), custom_call_target="tpu_custom_call" | custom-call | flops 8000000000 | bytes 20000000 | tf_op jit(solution)/shard_map/pallas_call | solution.py:364
  124.1 4.6 %add_bitcast_fusion = f32[1,384,2560]{2,1,0:T(8,128)} fusion(bf16[384,2560]{1,0:T(8,128)(2,1)} %get-tuple-element.8, bf16[384,2560]{1,0:T(8,128)(2,1)} %get-tuple-element.7), kind=kLoop, calls=%fused_computation | loop fusion | flops 2949120 | bytes 7864320 | tf_op jit(solution)/shard_map/broadcast_in_dim | solution.py:391

commit v4 on v3

--- a/solution.py
+++ b/solution.py
@@ -72,7 +72,7 @@
 
 def kernel(flags_ref, ids_hbm, num_hbm, tok_hbm, cot_hbm, wg_hbm, wu_hbm, sum_hbm, other_hbm,
            tok, cot, wg, wu, picked, hid, hid_other, hid_t, scaled, part, part_own, ids_ref, num_ref,
-           local_sem, z_send, z_recv, c_send, c_recv, d_send, d_recv, e_send, e_recv, o_sem,
+           local_sem, z_send, z_recv, c_send, c_recv, d_send, d_recv, o_sem,
            w_send, w_recv, h_send, h_recv, p_send, p_recv):
     rows, width = tok_hbm.shape
     count = ids_hbm.shape[0]
@@ -149,21 +149,16 @@
                       c_recv.at[a, way, s + 3], to_x if way == 0 else to_y)
 
     def d_copy(a, way, s, column):
-        size = rows // 2 if s == 0 else rows // 4
+        size = rows // 2
         start = (column * ZS + z + s) * rows + way * size
         return remote(arrays[a].at[pl.ds(pl.multiple_of(start, size), size)],
                       d_send.at[a, way, s + 3], d_recv.at[a, way, s + 3], to_x if way == 0 else to_y)
 
-    def e_copy(a, way, d, s):
-        start = (d_col * ZS + z + s) * rows + rows // 2
-        return remote(arrays[a].at[pl.ds(pl.multiple_of(start, rows // 2), rows // 2)],
-                      e_send.at[a, way, d], e_recv.at[a, way, d], up if way == 0 else down)
-
-    def z_sends(a, s, act, copy=z_copy):
+    def z_sends(a, s, act):
         if -3 < s <= 0:
-            pl.when(z < ZS - 1)(lambda: act(copy(a, 0, -s, s)))
+            pl.when(z < ZS - 1)(lambda: act(z_copy(a, 0, -s, s)))
         if 0 <= s < 3:
-            pl.when(z > 0)(lambda: act(copy(a, 1, s, s)))
+            pl.when(z > 0)(lambda: act(z_copy(a, 1, s, s)))
 
     def begin(copy):
         copy.start()
@@ -189,24 +184,12 @@
                 c_copy(a, 0, s, x_col).wait_recv()
                 d_copy(a, 1, s, x_col).start()
 
-    def step_e(a, d):
-        if d == 0:
-            d_copy(a, 1, 0, d_col).wait_recv()
-            z_sends(a, 0, begin, e_copy)
-            return
-        for s in (-d, d):
-            @pl.when(valid(s))
-            def _(s=s):
-                e_copy(a, 0 if s < 0 else 1, d - 1, s).wait_recv()
-                z_sends(a, s, begin, e_copy)
-
     def step_diagonal(a):
         for s in range(-3, 4):
             @pl.when(valid(s))
             def _(s=s):
                 d_copy(a, 0, s, d_col).wait_recv()
-                if s != 0:
-                    d_copy(a, 1, s, d_col).wait_recv()
+                d_copy(a, 1, s, d_col).wait_recv()
 
     chunk = ZS * rows
     packed = ZS * SLOTS
@@ -279,31 +262,26 @@
     step_z(0, 1)
     step_plane(0, 0)
     step_z(0, 2)
-    step_e(0, 0)
     z_sends(1, 0, begin)
     step_plane(0, 1)
     step_z(0, 3)
-    step_e(0, 1)
     loads[2].wait()
     loads[3].wait()
     remote(wg.at[1 - dp], w_send.at[0], w_recv.at[0], twin).wait_recv()
     remote(wu.at[1 - dp], w_send.at[1], w_recv.at[1], twin).wait_recv()
     hidden(0, col)
-    step_e(0, 2)
     step_plane(0, 2)
+    step_plane(0, 3)
     own_plane(1, 0)
-    step_plane(0, 3)
-    step_e(0, 3)
     step_z(1, 1)
     hidden(1, y_col)
+    step_z(1, 2)
     hidden(2, x_col)
-    step_z(1, 2)
     step_z(1, 3)
     step_diagonal(0)
     hidden(3, d_col)
     for d in range(4):
         step_plane(1, d)
-        step_e(1, d)
     for column in (col, y_col, x_col):
         scale(column)
     for k, column in enumerate((col, y_col, x_col, d_col)):
@@ -342,7 +320,6 @@
             @pl.when(valid(s))
             def _(a=a, s=s):
                 z_sends(a, s, lambda copy: copy.wait_send())
-                z_sends(a, s, lambda copy: copy.wait_send(), e_copy)
                 for way in range(2):
                     c_copy(a, way, s, col).wait_send()
                 d_copy(a, 0, s, y_col).wait_send()
@@ -381,7 +358,7 @@
             pltpu.VMEM((expert_ids.shape[1], rows), jnp.int32),
             pltpu.VMEM((expert_ids.shape[1], rows), jnp.int32),
             dma((6,)), dma((2, 2, 3)), dma((2, 2, 3)), dma((2, 2, 7)), dma((2, 2, 7)),
-            dma((2, 2, 7)), dma((2, 2, 7)), dma((2, 2, 3)), dma((2, 2, 3)), dma((TILES,)), dma((2,)), dma((2,)), dma((4,)), dma((4,)),
+            dma((2, 2, 7)), dma((2, 2, 7)), dma((TILES,)), dma((2,)), dma((2,)), dma((4,)), dma((4,)),
             dma((TILES,)), dma((TILES,)),
         ],
         compiler_params=pltpu.CompilerParams(

time: 129 us -> 106 us (0.82)
  Pallas kernels: 124 us -> 101 us
    pallas_call x1, Pallas kernels: 124 us -> 101 us  [fused(): pl.pallas_call(kernel, out_shape=[jax.ShapeDtypeStruct((ff // 2, width),...]
where the time goes in v4:
time: 106 us
  Pallas kernels  101 us (95%)
  other arithmetic  4.63 us (4%)
    pallas_call x1, Pallas kernels, fused(): pl.pallas_call(kernel, out_shape=[jax.ShapeDtypeStruct((ff // 2, width),...  101 us
    broadcast_in_dim x1, other arithmetic, fused(): return (term.astype(jnp.float32) + other.astype(jnp.float32))[None]  4.63 us

profile of v4, /device:TPU:0, one launch (start us, length us, event | category | flops | bytes accessed | tf_op | source)
XLA Modules:
  0.0 105.9 jit_solution(9478701026294110692)
XLA Ops:
  0.0 101.3 %shard_map.73 = (bf16[384,2560]{1,0:T(8,128)(2,1)}, bf16[384,2560]{1,0:T(8,128)(2,1)}) custom-call(s32[8]{0:T(128)} %flags_ref.1, s32[6,64]{1,0:T(8,128)} %bitcast.8, s32[6,64]{1,0:T(8,128)} %bitcast.9, bf16[64,2560]{1,0:T(8,128)(2,1)} %tok_hbm.1, bf16[64,2560]{1,0:T(8,128)(2,1)} %cot_hbm.1, bf16[1280,768]{1,0:T(8,128)(2,1)} %bitcast.6, ...), custom_call_target="tpu_custom_call" | custom-call | flops 8000000000 | bytes 20000000 | tf_op jit(solution)/shard_map/pallas_call | solution.py:341
  101.3 4.6 %add_bitcast_fusion = f32[1,384,2560]{2,1,0:T(8,128)} fusion(bf16[384,2560]{1,0:T(8,128)(2,1)} %get-tuple-element.8, bf16[384,2560]{1,0:T(8,128)(2,1)} %get-tuple-element.7), kind=kLoop, calls=%fused_computation | loop fusion | flops 2949120 | bytes 7864320 | tf_op jit(solution)/shard_map/broadcast_in_dim | solution.py:368

commit v5 on v4

--- a/solution.py
+++ b/solution.py
@@ -271,8 +271,8 @@
     remote(wu.at[1 - dp], w_send.at[1], w_recv.at[1], twin).wait_recv()
     hidden(0, col)
     step_plane(0, 2)
+    own_plane(1, 0)
     step_plane(0, 3)
-    own_plane(1, 0)
     step_z(1, 1)
     hidden(1, y_col)
     step_z(1, 2)

time: 106 us -> 106 us (level)
  no operation moved by 1% of the time
where the time goes in v5:
time: 106 us
  Pallas kernels  101 us (95%)
  other arithmetic  4.63 us (4%)
    pallas_call x1, Pallas kernels, fused(): pl.pallas_call(kernel, out_shape=[jax.ShapeDtypeStruct((ff // 2, width),...  101 us
    broadcast_in_dim x1, other arithmetic, fused(): return (term.astype(jnp.float32) + other.astype(jnp.float32))[None]  4.63 us

profile of v5, /device:TPU:0, one launch (start us, length us, event | category | flops | bytes accessed | tf_op | source)
XLA Modules:
  0.0 105.9 jit_solution(15637224211937082434)
XLA Ops:
  0.0 101.3 %shard_map.73 = (bf16[384,2560]{1,0:T(8,128)(2,1)}, bf16[384,2560]{1,0:T(8,128)(2,1)}) custom-call(s32[8]{0:T(128)} %flags_ref.1, s32[6,64]{1,0:T(8,128)} %bitcast.8, s32[6,64]{1,0:T(8,128)} %bitcast.9, bf16[64,2560]{1,0:T(8,128)(2,1)} %tok_hbm.1, bf16[64,2560]{1,0:T(8,128)(2,1)} %cot_hbm.1, bf16[1280,768]{1,0:T(8,128)(2,1)} %bitcast.6, ...), custom_call_target="tpu_custom_call" | custom-call | flops 8000000000 | bytes 20000000 | tf_op jit(solution)/shard_map/pallas_call | solution.py:341
  101.3 4.6 %add_bitcast_fusion = f32[1,384,2560]{2,1,0:T(8,128)} fusion(bf16[384,2560]{1,0:T(8,128)(2,1)} %get-tuple-element.8, bf16[384,2560]{1,0:T(8,128)(2,1)} %get-tuple-element.7), kind=kLoop, calls=%fused_computation | loop fusion | flops 2949120 | bytes 7864320 | tf_op jit(solution)/shard_map/broadcast_in_dim | solution.py:368
